TPU v7x, 512 devices: a whole 4x4x16 slice. The times are simulated.
512 devices in a mesh: occ: 8 (over x, core), vir: 64 (over z, y).
Axes of the slice: x: 4, y: 4, z: 16, core: 2. Of those that a mesh axis runs over, the one named last changes fastest.
Arguments:
- amplitudes: bfloat16 [3072, 128, 128], P('occ', 'vir'), may hold values from -6 to 6
- amp_blocks: int32 [128], P('vir'), may hold values from 0 to 255, as said below
- integrals: bfloat16 [64, 128, 128, 128], P('vir', 'occ'), may hold values from -0.125 to 0.125
- integral_rows: int32 [64, 128], P('vir', 'occ'), may hold values from -1 to 255, as said below
- integral_cols: int32 [64, 128], P('vir', 'occ'), may hold values from 0 to 255, as said below
Outputs:
- ladder: bfloat16 [3072, 256, 128], P('occ', 'vir')
Inputs may be any that keep to these rules, and one draw needn't show every extreme that they name: `amp_blocks`: distinct pair blocks. `integral_rows`: each entry is -1 (empty slot) or one of amp_blocks; live pairs (row, column) of one owner are distinct; one owner's live slots name each amplitude block at most once; every owner's slots have some live ones, and some owner has all 128 live. `integral_cols`: row v holds blocks v * 4 to v * 4 + 3.
All inputs are finite; a program needn't handle non-finite values.
Results may differ from a plain program's by a relative error of at most 0.0013.
Values may be sent and summed in bfloat16 or wider, within the bound.
A program may use at most 128 MiB of HBM per device.

v0:
```python
import math

import jax
import jax.numpy as jnp
from jax import lax
from jax.sharding import PartitionSpec as P

OBLK = 4


def locate(wanted, known):
    index = jnp.arange(known.shape[0], dtype=jnp.int32)
    match = wanted[:, None] == known[None, :]
    return jnp.sum(jnp.where(match, index[None, :], 0), axis=1)


def tile_terms(source, slots, tile_mats, local_cols, valid, blocks):
    picked = jnp.take(source, slots, axis=1)
    product = jnp.einsum("rkt,ktu->rku", picked, tile_mats, preferred_element_type=jnp.float32)
    columns = jnp.arange(blocks, dtype=jnp.int32)
    onehot = ((local_cols[:, None] == columns[None, :]) & valid[:, None]).astype(jnp.float32)
    return jnp.einsum("rku,kc->rcu", product, onehot, precision=lax.Precision.HIGHEST)


def on_device(amplitudes, amp_blocks, integrals, integral_rows, integral_cols):
    rows, aslot, tile = amplitudes.shape
    owner = lax.axis_index("vir")
    known = lax.all_gather(amp_blocks, "vir", axis=0, tiled=True)
    total = jnp.zeros((rows, OBLK, tile), jnp.float32)
    whole = lax.all_gather(amplitudes, "vir", axis=1, tiled=True)
    tiles = lax.all_gather(integrals, "occ", axis=1, tiled=True)
    prow = lax.all_gather(integral_rows, "occ", axis=1, tiled=True)
    pcol = lax.all_gather(integral_cols, "occ", axis=1, tiled=True)
    tiles = tiles[0]
    prow = prow[0]
    pcol = pcol[0]
    count = prow.shape[0]
    group = math.gcd(count, 16)
    slots = locate(prow, known)
    packed = (
        tiles.reshape(count // group, group, tile, tile),
        slots.reshape(count // group, group),
        (pcol - owner * OBLK).reshape(count // group, group),
        (prow >= 0).reshape(count // group, group),
    )

    def step(acc, item):
        tile_mats, slot_part, col_part, valid_part = item
        return (acc + tile_terms(whole, slot_part, tile_mats, col_part, valid_part, OBLK), None)

    result, unused = lax.scan(step, total, packed)
    total = result
    return total.astype(jnp.bfloat16)


def solution(mesh):
    return jax.shard_map(
        on_device,
        mesh=mesh,
        in_specs=(
            P("occ", "vir", None),
            P("vir"),
            P("vir", "occ", None, None),
            P("vir", "occ"),
            P("vir", "occ"),
        ),
        out_specs=P("occ", "vir", None),
        check_vma=False,
    )
```

profile of v0, /device:TPU:1, one launch (start us, length us, event | category | flops | bytes accessed | tf_op | source)
XLA Modules:
  0.0 360.0 jit_solution(15437157085576815567)
XLA Ops:
  13.7 29.8 %all-reduce.2 = s32[128]{0:T(128)S(1)} all-reduce(s32[128]{0:T(128)S(1)} %dynamic-update-slice.2), channel_id=1, replica_groups=mesh['occ'=8,'vir'=64] {'vir'}, use_global_device_ids=true, to_apply=%add.2 | all-reduce | flops 128 | bytes 1024
  45.0 12.9 %all-reduce.3 = (s32[128]{0:T(128)S(1)}, s32[128]{0:T(128)S(1)}) all-reduce(s32[128]{0:T(128)S(1)} %bitcast_dynamic-update-slice_fusion.1, s32[128]{0:T(128)S(1)} %bitcast_dynamic-update-slice_fusion), channel_id=1, replica_groups=mesh['occ'=8,'vir'=64] {'occ'}, use_global_device_ids=true, to_apply=%add | all-reduce | flops 256 | bytes 2048
  58.3 168.5 %all-gather.5.cloned.1.call-done = bf16[384,128,128]{2,0,1:T(8,128)(2,1)} async-done(((bf16[384,2,128]{2,0,1:T(8,128)(2,1)}), bf16[384,128,128]{2,0,1:T(8,128)(2,1)}) %all-gather.5.cloned.1.call-update) | async-done | bytes 12582928 | tf_op jit(solution)/shard_map/all_gather | solution.py:30
  226.8 124.4 %while.11 = (s32[]{:T(128)}, f32[384,4,128]{2,1,0:T(4,128)}, s32[8,16]{1,0:T(8,128)S(1)}, pred[8,16]{1,0:T(8,128)(4,1)S(1)}, bf16[8,16,128,128]{3,2,1,0:T(8,128)...) while((s32[]{:T(128)}, f32[384,4,128]{2,1,0:T(4,128)}, ...), condition=%wide.region_2.3_spmd.clone, body=%wide.region_1.2_spmd.clone.sunk | while | flops 240256272 | bytes 19403976 | solution.py:51
  226.8 6.5 %gather_fusion = bf16[16,384,128]{2,1,0:T(8,128)(2,1)} fusion(bf16[384,128,128]{2,0,1:T(8,128)(2,1)} %get-tuple-element.164, s32[1024]{0:T(1024)S(1)} %pad_clamp_fusion.2), kind=kCustom, calls=%fused_computation.clone.clone.1 | custom fusion | bytes 3145792 | tf_op jit(solution)/shard_map/while/body/eval_jaxpr/jit(_take)/gather | solution.py:18
  235.7 2.4 copy.17
  238.1 4.1 %fusion.30 = f32[384,4,128]{2,1,0:T(4,128)} fusion(f32[384,16,128]{2,1,0:T(8,128)} %copy.17, f32[384,4,128]{2,1,0:T(4,128)} %get-tuple-element.150, pred[]{:T(512)S(6)} %compare.3, s32[16]{0:T(128)S(1)} %fusion.29, pred[16]{0:T(512)(128)(4,1)S(1)} %dynamic-slice_bitcast_fusion.2), kind=kOutput, calls=%fused_computation.6.clone.1 | convolution fusion | flops 38142080 | bytes 4718673 | tf_op jit(solution)/shard_map/while/body/eval_jaxpr/rku,kc->rcu/dot_general | solution.py:22
  242.2 6.5 %gather_fusion = bf16[16,384,128]{2,1,0:T(8,128)(2,1)} fusion(bf16[384,128,128]{2,0,1:T(8,128)(2,1)} %get-tuple-element.164, s32[1024]{0:T(1024)S(1)} %pad_clamp_fusion.2), kind=kCustom, calls=%fused_computation.clone.clone.1 | custom fusion | bytes 3145792 | tf_op jit(solution)/shard_map/while/body/eval_jaxpr/jit(_take)/gather | solution.py:18
  251.1 2.4 copy.17
  253.5 4.3 %fusion.30 = f32[384,4,128]{2,1,0:T(4,128)} fusion(f32[384,16,128]{2,1,0:T(8,128)} %copy.17, f32[384,4,128]{2,1,0:T(4,128)} %get-tuple-element.150, pred[]{:T(512)S(6)} %compare.3, s32[16]{0:T(128)S(1)} %fusion.29, pred[16]{0:T(512)(128)(4,1)S(1)} %dynamic-slice_bitcast_fusion.2), kind=kOutput, calls=%fused_computation.6.clone.1 | convolution fusion | flops 38142080 | bytes 4718673 | tf_op jit(solution)/shard_map/while/body/eval_jaxpr/rku,kc->rcu/dot_general | solution.py:22
  257.8 6.5 %gather_fusion = bf16[16,384,128]{2,1,0:T(8,128)(2,1)} fusion(bf16[384,128,128]{2,0,1:T(8,128)(2,1)} %get-tuple-element.164, s32[1024]{0:T(1024)S(1)} %pad_clamp_fusion.2), kind=kCustom, calls=%fused_computation.clone.clone.1 | custom fusion | bytes 3145792 | tf_op jit(solution)/shard_map/while/body/eval_jaxpr/jit(_take)/gather | solution.py:18
  266.6 2.4 copy.17
  269.1 4.3 %fusion.30 = f32[384,4,128]{2,1,0:T(4,128)} fusion(f32[384,16,128]{2,1,0:T(8,128)} %copy.17, f32[384,4,128]{2,1,0:T(4,128)} %get-tuple-element.150, pred[]{:T(512)S(6)} %compare.3, s32[16]{0:T(128)S(1)} %fusion.29, pred[16]{0:T(512)(128)(4,1)S(1)} %dynamic-slice_bitcast_fusion.2), kind=kOutput, calls=%fused_computation.6.clone.1 | convolution fusion | flops 38142080 | bytes 4718673 | tf_op jit(solution)/shard_map/while/body/eval_jaxpr/rku,kc->rcu/dot_general | solution.py:22
  273.3 6.5 %gather_fusion = bf16[16,384,128]{2,1,0:T(8,128)(2,1)} fusion(bf16[384,128,128]{2,0,1:T(8,128)(2,1)} %get-tuple-element.164, s32[1024]{0:T(1024)S(1)} %pad_clamp_fusion.2), kind=kCustom, calls=%fused_computation.clone.clone.1 | custom fusion | bytes 3145792 | tf_op jit(solution)/shard_map/while/body/eval_jaxpr/jit(_take)/gather | solution.py:18
  282.2 2.4 copy.17
  284.6 4.3 %fusion.30 = f32[384,4,128]{2,1,0:T(4,128)} fusion(f32[384,16,128]{2,1,0:T(8,128)} %copy.17, f32[384,4,128]{2,1,0:T(4,128)} %get-tuple-element.150, pred[]{:T(512)S(6)} %compare.3, s32[16]{0:T(128)S(1)} %fusion.29, pred[16]{0:T(512)(128)(4,1)S(1)} %dynamic-slice_bitcast_fusion.2), kind=kOutput, calls=%fused_computation.6.clone.1 | convolution fusion | flops 38142080 | bytes 4718673 | tf_op jit(solution)/shard_map/while/body/eval_jaxpr/rku,kc->rcu/dot_general | solution.py:22
  288.9 6.5 %gather_fusion = bf16[16,384,128]{2,1,0:T(8,128)(2,1)} fusion(bf16[384,128,128]{2,0,1:T(8,128)(2,1)} %get-tuple-element.164, s32[1024]{0:T(1024)S(1)} %pad_clamp_fusion.2), kind=kCustom, calls=%fused_computation.clone.clone.1 | custom fusion | bytes 3145792 | tf_op jit(solution)/shard_map/while/body/eval_jaxpr/jit(_take)/gather | solution.py:18
  300.2 4.3 %fusion.30 = f32[384,4,128]{2,1,0:T(4,128)} fusion(f32[384,16,128]{2,1,0:T(8,128)} %copy.17, f32[384,4,128]{2,1,0:T(4,128)} %get-tuple-element.150, pred[]{:T(512)S(6)} %compare.3, s32[16]{0:T(128)S(1)} %fusion.29, pred[16]{0:T(512)(128)(4,1)S(1)} %dynamic-slice_bitcast_fusion.2), kind=kOutput, calls=%fused_computation.6.clone.1 | convolution fusion | flops 38142080 | bytes 4718673 | tf_op jit(solution)/shard_map/while/body/eval_jaxpr/rku,kc->rcu/dot_general | solution.py:22
  304.5 6.5 %gather_fusion = bf16[16,384,128]{2,1,0:T(8,128)(2,1)} fusion(bf16[384,128,128]{2,0,1:T(8,128)(2,1)} %get-tuple-element.164, s32[1024]{0:T(1024)S(1)} %pad_clamp_fusion.2), kind=kCustom, calls=%fused_computation.clone.clone.1 | custom fusion | bytes 3145792 | tf_op jit(solution)/shard_map/while/body/eval_jaxpr/jit(_take)/gather | solution.py:18
  315.8 4.3 %fusion.30 = f32[384,4,128]{2,1,0:T(4,128)} fusion(f32[384,16,128]{2,1,0:T(8,128)} %copy.17, f32[384,4,128]{2,1,0:T(4,128)} %get-tuple-element.150, pred[]{:T(512)S(6)} %compare.3, s32[16]{0:T(128)S(1)} %fusion.29, pred[16]{0:T(512)(128)(4,1)S(1)} %dynamic-slice_bitcast_fusion.2), kind=kOutput, calls=%fused_computation.6.clone.1 | convolution fusion | flops 38142080 | bytes 4718673 | tf_op jit(solution)/shard_map/while/body/eval_jaxpr/rku,kc->rcu/dot_general | solution.py:22
  320.1 6.5 %gather_fusion = bf16[16,384,128]{2,1,0:T(8,128)(2,1)} fusion(bf16[384,128,128]{2,0,1:T(8,128)(2,1)} %get-tuple-element.164, s32[1024]{0:T(1024)S(1)} %pad_clamp_fusion.2), kind=kCustom, calls=%fused_computation.clone.clone.1 | custom fusion | bytes 3145792 | tf_op jit(solution)/shard_map/while/body/eval_jaxpr/jit(_take)/gather | solution.py:18
  331.3 4.3 %fusion.30 = f32[384,4,128]{2,1,0:T(4,128)} fusion(f32[384,16,128]{2,1,0:T(8,128)} %copy.17, f32[384,4,128]{2,1,0:T(4,128)} %get-tuple-element.150, pred[]{:T(512)S(6)} %compare.3, s32[16]{0:T(128)S(1)} %fusion.29, pred[16]{0:T(512)(128)(4,1)S(1)} %dynamic-slice_bitcast_fusion.2), kind=kOutput, calls=%fused_computation.6.clone.1 | convolution fusion | flops 38142080 | bytes 4718673 | tf_op jit(solution)/shard_map/while/body/eval_jaxpr/rku,kc->rcu/dot_general | solution.py:22
  335.6 6.5 %gather_fusion = bf16[16,384,128]{2,1,0:T(8,128)(2,1)} fusion(bf16[384,128,128]{2,0,1:T(8,128)(2,1)} %get-tuple-element.164, s32[1024]{0:T(1024)S(1)} %pad_clamp_fusion.2), kind=kCustom, calls=%fused_computation.clone.clone.1 | custom fusion | bytes 3145792 | tf_op jit(solution)/shard_map/while/body/eval_jaxpr/jit(_take)/gather | solution.py:18
  346.9 4.3 %fusion.30 = f32[384,4,128]{2,1,0:T(4,128)} fusion(f32[384,16,128]{2,1,0:T(8,128)} %copy.17, f32[384,4,128]{2,1,0:T(4,128)} %get-tuple-element.150, pred[]{:T(512)S(6)} %compare.3, s32[16]{0:T(128)S(1)} %fusion.29, pred[16]{0:T(512)(128)(4,1)S(1)} %dynamic-slice_bitcast_fusion.2), kind=kOutput, calls=%fused_computation.6.clone.1 | convolution fusion | flops 38142080 | bytes 4718673 | tf_op jit(solution)/shard_map/while/body/eval_jaxpr/rku,kc->rcu/dot_general | solution.py:22
  (74 shorter events, 38.6 us)
Async XLA Ops:
  6.5 51.7 %all-gather.3.cloned.1.call-start = ((), (), s32[]{:S(2)}) async-start(), calls=%async_computation | async-start | bytes 4718592 | tf_op jit(solution)/shard_map/all_gather | solution.py:31
  7.3 219.5 %all-gather.5.cloned.1.call-start = ((), (), s32[]{:S(2)}) async-start(), calls=%async_computation.1 | async-start | bytes 12779520 | tf_op jit(solution)/shard_map/all_gather | solution.py:30
Sparse Core Ops, SparseCore 0:
  9.5 45.4 all-gather.2
  58.0 168.7 all-gather.4
where the time goes:
time: 362 us; the launch traced here: 360 us
  waiting for transfers between devices  169 us (47%)
  local copies, waits for them, and re-layouts  78.1 us (22%)
  matrix products  52.8 us (15%)
  blocking collectives  42.6 us (12%)
  between operations  14.7 us (4%)
    all_gather x1, waiting for transfers between devices, on_device(): whole = lax.all_gather(amplitudes, 'vir', axis=1, tiled=True)  169 us
    gather x8, local copies, waits for them, and re-layouts, tile_terms(): picked = jnp.take(source, slots, axis=1)  51.8 us
    unnamed x2, blocking collectives  42.6 us
    dot_general x8, matrix products, tile_terms(): jnp.einsum('rku,kc->rcu', product, onehot, precision=lax.Precision.HIGHEST)  33.9 us
    transpose x8, local copies, waits for them, and re-layouts, tile_terms(): jnp.einsum('rkt,ktu->rku', picked, tile_mats, preferred_element_type=jnp....  19.3 us
    dot_general x8, matrix products, tile_terms(): jnp.einsum('rkt,ktu->rku', picked, tile_mats, preferred_element_type=jnp....  18.9 us
  transfers between devices with their start and end apart: 2, of which 1 were waited for; matrix products, arithmetic and copies ran while one was open for 2% of the time, Pallas kernels for 0%

commit v1 on v0

v1 whole, which is shorter than its diff:
```python
import functools

import jax
import jax.numpy as jnp
from jax import lax
from jax.experimental import pallas as pl
from jax.experimental.pallas import tpu as pltpu
from jax.sharding import PartitionSpec as P

MESH = pl.DeviceIdType.MESH
OBLK = 4
TILE = 128
NX, NY, NZ = 4, 4, 16
SUB = 96
CHUNK = 8
NS = 128
GROUPS = ((0, 0), (0, 1), (0, 3), (1, 0), (0, 2), (1, 1), (1, 3), (1, 2))


def kernel(
    a_in, w_in, blocks, rows, cols, out_ref,
    a_src, a_all, id_all, w_all, wi_all, acc, wide, stage, id_own, wi_own, merged, info, table,
    a0_send, a0_recv, z_send, z_recv, zi_send, zi_recv, d_send, d_recv,
    own_send, owni_send, w_recv, wi_recv, f_send, fi_send, out_send, out_recv, info_sem,
):
    occ, vir = lax.axis_index("occ"), lax.axis_index("vir")
    x, c = occ // 2, lax.rem(occ, 2)
    z, y = vir // NY, lax.rem(vir, NY)
    home = y // 2
    unmatched = (c + home) % 2
    oy = lax.rem(y, 2)

    def dev(xx, cc, yy, zz):
        return (lax.rem(xx + NX, NX) * 2 + cc, lax.rem(zz + NZ, NZ) * NY + lax.rem(yy + NY, NY))

    def remote(src, dst, send, recv, device):
        return pltpu.make_async_remote_copy(
            src_ref=src, dst_ref=dst, send_sem=send, recv_sem=recv, device_id=device, device_id_type=MESH
        )

    def landed(ref, sem):
        pltpu.make_async_copy(ref, ref, sem).wait()

    partners = [dev(x, (c + k) % 2, y + j, z) for j in range(NY) for k in range(2) if (j, k) != (0, 0)]
    partners += [dev(x + s, k, y, z) for s in (1, -1) for k in range(2)]
    partners += [dev(x, c, y, z + s) for s in (1, -1)]
    barrier = pltpu.get_barrier_semaphore()
    for p in partners:
        pl.semaphore_signal(barrier, inc=1, device_id=p, device_id_type=MESH)

    wide[...] = a_in[...].astype(jnp.float32)
    for b in range(2):
        a_src[b] = wide[pl.ds(b, NY * SUB, stride=2), :].astype(jnp.bfloat16)
    sub = lax.broadcasted_iota(jnp.int32, (8, TILE), 0)
    lane = lax.broadcasted_iota(jnp.int32, (8, TILE), 1)
    place_of = sub * TILE + lane
    mark = jnp.zeros((8, TILE), jnp.int32)
    for b in range(2):
        mark = jnp.where(place_of == blocks[b], 2 * vir + b, mark)
    id_own[...] = mark
    mark = jnp.zeros((8, TILE), jnp.int32)
    for t in range(2 * CHUNK):
        here = lane == occ * 2 * CHUNK + t
        mark = jnp.where(here & (sub == 2), rows[0, t], mark)
        local = jnp.where(rows[0, t] >= 0, cols[0, t] - vir * OBLK, OBLK)
        mark = jnp.where(here & (sub == 3), local, mark)
    wi_own[...] = mark
    acc[...] = jnp.zeros_like(acc)

    pl.semaphore_wait(barrier, len(partners))

    a_local = []
    for b in range(2):
        a_local.append(pltpu.make_async_copy(a_src.at[b, pl.ds(y * SUB, SUB)], a_all.at[c, 2 * vir + b], a0_recv.at[0, b]))
    a_local.append(pltpu.make_async_copy(id_own, id_all.at[vir], a0_recv.at[0, 2]))
    for copy in a_local:
        copy.start()
    a0 = []
    for k in (1, 3, 2):
        to = lax.rem(y + k, NY)
        for b in range(2):
            src = a_src.at[b, pl.ds(to * SUB, SUB)]
            a0.append(remote(src, a_all.at[c, 2 * vir + b], a0_send.at[k, b], a0_recv.at[k, b], dev(x, c, to, z)))
        a0.append(remote(id_own, id_all.at[vir], a0_send.at[k, 2], a0_recv.at[k, 2], dev(x, c, to, z)))
    for copy in a0:
        copy.start()

    mine, mine_sem = w_all.at[oy, x, c], w_recv.at[oy, x, c]
    targets = (dev(x + 1, home, y, z), dev(x - 1, home, y, z), dev(x, home, y + 1, z), dev(x, home, y - 1, z))
    beside = dev(x, home, y, z)
    w_src = [w_in.at[0, pl.ds(r * CHUNK, CHUNK)] for r in range(2)]

    def own_tiles(r, d, to):
        return remote(w_src[r], mine.at[r], own_send.at[r, d], mine_sem.at[r], to)

    def own_marks(d, to):
        return remote(wi_own, wi_all.at[oy, x, c], owni_send.at[d], wi_recv.at[oy, x, c], to)

    def own_start(ds):
        for r in range(2):
            for d in ds:
                own_tiles(r, d, targets[d]).start()
                if r == 0:
                    own_marks(d, targets[d]).start()

    def own_beside():
        @pl.when(unmatched == 0)
        def _():
            for r in range(2):
                pltpu.make_async_copy(w_src[r], mine.at[r], mine_sem.at[r]).start()
            pltpu.make_async_copy(wi_own, wi_all.at[oy, x, c], wi_recv.at[oy, x, c]).start()

        @pl.when(unmatched == 1)
        def _():
            for r in range(2):
                own_tiles(r, 4, beside).start()
            own_marks(4, beside).start()

    def zchunk(ref, zz, lo, n, per):
        return ref.at[pl.ds(lax.rem(zz + NZ, NZ) * per + lo, n)]

    def plan(way, h):
        return [way] if h == NZ // 2 else [0, 1]

    def z_copy(way, h, q, arriving=False):
        s = 1 if way == 0 else -1
        from_z = z - s * (h if arriving else h - 1)
        to = dev(x, c, y, z + s)
        chunk = zchunk(a_all.at[c], from_z, 4 * q, 4, 2 * NY)
        out = [remote(chunk, chunk, z_send.at[way, q, h - 1], z_recv.at[way, q, h - 1], to)]
        if q == 0:
            chunk = zchunk(id_all, from_z, 0, NY, NY)
            out.append(remote(chunk, chunk, zi_send.at[way, h - 1], zi_recv.at[way, h - 1], to))
        return out

    def d_copy(way, h, core, q):
        s = 1 if way == 0 else -1
        chunk = zchunk(a_all.at[core], z - s * h, 4 * q, 4, 2 * NY)
        return remote(chunk, chunk, d_send.at[way, q, h], d_recv.at[way, q, h], dev(x, 1 - c, y, z))

    def z_step(h):
        for q in range(2):
            for way in range(2):
                if q not in plan(way, h):
                    continue
                for copy in z_copy(way, h, q, arriving=True):
                    copy.wait_recv()
                if h < NZ // 2 and q in plan(way, h + 1):
                    for copy in z_copy(way, h + 1, q):
                        copy.start()
                d_copy(way, h, c, q).start()

    nearest = (oy + unmatched) % 2

    def forwards(j, dx, cs, r):
        o = nearest if j == 0 else 1 - nearest
        xs = lax.rem(x - dx + NX, NX)
        dy = lax.rem(y - (2 * c + o) + NY, NY)
        slot, sem = w_all.at[o, xs, cs, r], w_recv.at[o, xs, cs, r]
        marks, marks_sem = wi_all.at[o, xs, cs], wi_recv.at[o, xs, cs]

        def send(d):
            to = (dev(x + 1, c, y, z), dev(x - 1, c, y, z), dev(x, c, y + 1, z), dev(x, c, y - 1, z))[d]
            out = [remote(slot, slot, f_send.at[j, dx, cs, r, d], sem, to)]
            if r == 0:
                out.append(remote(marks, marks, fi_send.at[j, dx, cs, d], marks_sem, to))
            return out

        on_x = (0,) if (dx == 1 and cs == 0) else (1,) if (dx == 3 and cs == 1) else ()
        dy_on = 1 if cs == 0 else 3
        todo = []
        if r == 0:
            if dx != 0:
                todo.append((dy == 0, sum([send(d) for d in on_x + (2, 3)], [])))
            todo.append((dy == dy_on, send(2 + cs)))
        else:
            if dx == 0:
                todo.append((dy == dy_on, send(2 + cs)))
                todo.append((dy != 0, send(0) + send(1)))
            elif on_x:
                todo.append((None, sum([send(d) for d in on_x], [])))
        return todo

    def each(todo, act):
        for cond, copies in todo:

            def run(copies=copies):
                for copy in copies:
                    act(copy)

            if cond is None:
                run()
            else:
                pl.when(cond)(run)

    def group(g):
        j, dx = GROUPS[g]
        o = nearest if j == 0 else 1 - nearest
        xs = lax.rem(x - dx + NX, NX)
        for r in range(2):
            for cs in range(2):
                landed(w_all.at[o, xs, cs, r], w_recv.at[o, xs, cs, r])
                if r == 0:
                    landed(wi_all.at[o, xs, cs], wi_recv.at[o, xs, cs])
                each(forwards(j, dx, cs, r), lambda copy: copy.start())

    def groups(which, *gs):
        @pl.when(unmatched == which)
        def _():
            for g in gs:
                group(g)

    def product(o, p):
        marks = table[...]
        for i in range(NX * 2):
            marks = marks + wi_all[o, i // 2, i % 2]
        merged[p] = marks
        copy = pltpu.make_async_copy(merged.at[p], info.at[p], info_sem.at[p])
        copy.start()
        copy.wait()

        def chunk(i, carry):
            lhs, rhs = [], []
            for t in range(CHUNK):
                row = jnp.maximum(info[p, 2, i * CHUNK + t], 0)
                col = info[p, 3, i * CHUNK + t]
                s = jnp.minimum(info[p, row // TILE, row % TILE], NS - 1)
                lhs.append(jnp.concatenate([a_all[k, s] for k in range(2)], axis=0))
                tile = w_all[o, i // 4, (i // 2) % 2, i % 2, t]
                rhs.append(jnp.concatenate([jnp.where(col == b, tile, jnp.zeros_like(tile)) for b in range(OBLK)], axis=1))
            left = jnp.concatenate(lhs, axis=1)
            right = jnp.concatenate(rhs, axis=0)
            acc[o] += jnp.dot(left, right, preferred_element_type=jnp.float32)
            return carry

        lax.fori_loop(0, NX * 4, chunk, 0)

    def out_copies(o, p, act):
        ys = 2 * c + o
        for k in range(2):
            src, dst, sem = stage.at[p, k], out_ref.at[pl.ds(y * SUB * OBLK, SUB * OBLK)], out_recv.at[y]
            here = (ys == y) & (k == c)

            @pl.when(here)
            def _():
                act(pltpu.make_async_copy(src, dst, sem), True)

            @pl.when(jnp.logical_not(here))
            def _():
                act(remote(src, dst, out_send.at[p, k], sem, dev(x, k, ys, z)), False)

    def finish(o, p):
        for k in range(2):
            for b in range(OBLK):
                wide[pl.ds(b, SUB, stride=OBLK), :] = acc[o, pl.ds(k * SUB, SUB), pl.ds(b * TILE, TILE)]
            stage[p, k] = wide[pl.ds(0, SUB * OBLK), :].astype(jnp.bfloat16)
        out_copies(o, p, lambda copy, local: copy.start())

    own_start((0, 1))
    own_beside()
    for copy in a_local:
        copy.wait()
    for k in (1, 3, 2):
        from_y = lax.rem(y - k + NY, NY) + z * NY
        for b in range(2):
            landed(a_all.at[c, 2 * from_y + b], a0_recv.at[k, b])
        landed(id_all.at[from_y], a0_recv.at[k, 2])
    for q in range(2):
        for way in range(2):
            for copy in z_copy(way, 1, q):
                copy.start()
    own_start((2, 3))
    for q in range(2):
        d_copy(0, 0, c, q).start()

    groups(0, 0)
    z_step(1)
    groups(0, 1, 2, 3)
    groups(1, 0)
    for h in (2, 3, 4, 5):
        z_step(h)
    groups(0, 4, 5, 6)
    groups(1, 1, 2, 3)
    z_step(6)
    z_step(7)
    groups(0, 7)
    groups(1, 4, 5, 6)
    z_step(8)
    for q in range(2):
        d_copy(0, 0, 1 - c, q).wait_recv()
        for h in range(1, NZ // 2 + 1):
            for way in range(2):
                if q in plan(way, h):
                    d_copy(way, h, 1 - c, q).wait_recv()

    table[...] = lax.fori_loop(0, NY * NZ, lambda i, total: total + id_all[i], jnp.zeros((8, TILE), jnp.int32))
    first = (nearest + 1 - unmatched) % 2
    product(first, 0)
    finish(first, 0)
    groups(1, 7)
    product(1 - first, 1)
    finish(1 - first, 1)

    for copy in a0:
        copy.wait_send()
    for r in range(2):
        for d in range(4):
            own_tiles(r, d, targets[d]).wait_send()
            if r == 0:
                own_marks(d, targets[d]).wait_send()

    @pl.when(unmatched == 1)
    def _():
        for r in range(2):
            own_tiles(r, 4, beside).wait_send()
        own_marks(4, beside).wait_send()

    for q in range(2):
        d_copy(0, 0, c, q).wait_send()
        for h in range(1, NZ // 2 + 1):
            for way in range(2):
                if q in plan(way, h):
                    for copy in z_copy(way, h, q):
                        copy.wait_send()
                    d_copy(way, h, c, q).wait_send()
    for j, dx in GROUPS:
        for r in range(2):
            for cs in range(2):
                each(forwards(j, dx, cs, r), lambda copy: copy.wait_send())
    for o, p in ((first, 0), (1 - first, 1)):
        out_copies(o, p, lambda copy, local: None if local else copy.wait_send())
    for k in range(NY):
        landed(out_ref.at[pl.ds(k * SUB * OBLK, SUB * OBLK)], out_recv.at[k])


def on_device(amplitudes, amp_blocks, integrals, integral_rows, integral_cols):
    rows, aslot, tile = amplitudes.shape
    dma, half, vmem, smem = pltpu.SemaphoreType.DMA, NZ // 2, pltpu.VMEM, pltpu.SMEM
    out = pl.pallas_call(
        kernel,
        out_shape=jax.ShapeDtypeStruct((rows * OBLK, tile), jnp.bfloat16),
        in_specs=[
            pl.BlockSpec(memory_space=vmem),
            pl.BlockSpec(memory_space=pl.ANY),
            pl.BlockSpec(memory_space=smem),
            pl.BlockSpec(memory_space=smem),
            pl.BlockSpec(memory_space=smem),
        ],
        out_specs=pl.BlockSpec(memory_space=vmem),
        scratch_shapes=[
            vmem((2, NY * SUB, tile), jnp.bfloat16),
            vmem((2, NS, SUB, tile), jnp.bfloat16),
            vmem((NY * NZ, 8, tile), jnp.int32),
            vmem((2, NX, 2, 2, CHUNK, tile, tile), jnp.bfloat16),
            vmem((2, NX, 2, 8, tile), jnp.int32),
            vmem((2, 2 * SUB, OBLK * tile), jnp.float32),
            vmem((2 * rows, tile), jnp.float32),
            vmem((2, 2, SUB * OBLK, tile), jnp.bfloat16),
            vmem((8, tile), jnp.int32),
            vmem((8, tile), jnp.int32),
            vmem((2, 8, tile), jnp.int32),
            smem((2, 8, tile), jnp.int32),
            vmem((8, tile), jnp.int32),
            dma((NY, 3)), dma((NY, 3)),
            dma((2, 2, half)), dma((2, 2, half)), dma((2, half)), dma((2, half)),
            dma((2, 2, half + 1)), dma((2, 2, half + 1)),
            dma((2, 5)), dma((5,)), dma((2, NX, 2, 2)), dma((2, NX, 2)),
            dma((2, NX, 2, 2, 4)), dma((2, NX, 2, 4)),
            dma((2, 2)), dma((NY,)), dma((2,)),
        ],
        compiler_params=pltpu.CompilerParams(
            collective_id=0, has_side_effects=True, vmem_limit_bytes=56 << 20
        ),
    )(amplitudes.reshape(rows * aslot, tile), integrals, amp_blocks, integral_rows, integral_cols)
    return out.reshape(rows, OBLK, tile)


def solution(mesh):
    return jax.shard_map(
        on_device,
        mesh=mesh,
        in_specs=(
            P("occ", "vir", None),
            P("vir"),
            P("vir", "occ", None, None),
            P("vir", "occ"),
            P("vir", "occ"),
        ),
        out_specs=P("occ", "vir", None),
        check_vma=False,
    )
```

time: 362 us -> 91.6 us (0.25)
  waiting for transfers between devices: 169 us -> 0 us
  Pallas kernels: 0 us -> 89.6 us
  local copies, waits for them, and re-layouts: 78.1 us -> 1.88 us
  matrix products: 52.8 us -> 0 us
  blocking collectives: 42.6 us -> 0 us
  between operations: 14.7 us -> 0.01 us
    all_gather x2 -> x0, waiting for transfers between devices: 169 us -> none  [the longest x1 169 us: on_device(): whole = lax.all_gather(amplitudes, 'vir', axis=1, tiled=True)]
    pallas_call x0 -> x1, Pallas kernels: none -> 89.6 us  [on_device(): pl.pallas_call(kernel, out_shape=jax.ShapeDtypeStruct((rows * OBLK, tile)...]
    dot_general x16 -> x0, matrix products: 52.8 us -> none  [the longest x8 33.9 us: tile_terms(): jnp.einsum('rku,kc->rcu', product, onehot, precision=lax.Precision.HIGHEST)]
    gather x8 -> x0, local copies, waits for them, and re-layouts: 51.8 us -> none  [tile_terms(): picked = jnp.take(source, slots, axis=1)]
    unnamed x2 -> x0, blocking collectives: 42.6 us -> none
    transpose x8 -> x0, local copies, waits for them, and re-layouts: 19.3 us -> none  [tile_terms(): jnp.einsum('rkt,ktu->rku', picked, tile_mats, preferred_element_type=jnp....]
    unnamed x9 -> x1, local copies, waits for them, and re-layouts: 6.58 us -> 1.88 us
  transfers between devices with their start and end apart: 2 -> 0, of which waited for: 1 -> 0; matrix products, arithmetic and copies ran while one was open for 2% -> 0% of each run, Pallas kernels for 0% -> 0%
where the time goes in v1:
time: 91.6 us; the launch traced here: 91.5 us
  Pallas kernels  89.6 us (98%)
  local copies, waits for them, and re-layouts  1.88 us (2%)
    pallas_call x1, Pallas kernels, on_device(): pl.pallas_call(kernel, out_shape=jax.ShapeDtypeStruct((rows * OBLK, tile)...  89.6 us
    unnamed x1, local copies, waits for them, and re-layouts  1.88 us

profile of v1, /device:TPU:1, one launch (start us, length us, event | category | flops | bytes accessed | tf_op | source)
XLA Modules:
  0.0 91.5 jit_solution(7828874462750868541)
XLA Ops:
  0.0 89.6 %shard_map.55 = bf16[1536,128]{1,0:T(8,128)(2,1)} custom-call(bf16[768,128]{1,0:T(8,128)(2,1)} %bitcast.3, bf16[1,16,128,128]{3,2,1,0:T(8,128)(2,1)} %w_in.1, s32[2]{0:T(128)} %blocks.1, s32[1,16]{1,0:T(1,128)} %rows.1, s32[1,16]{1,0:T(1,128)} %cols.1), custom_call_target="tpu_custom_call" | custom-call | tf_op jit(solution)/shard_map/pallas_call | solution.py:339
  89.6 1.9 %copy.7 = bf16[384,4,128]{2,1,0:T(4,128)(2,1)} copy(bf16[384,4,128]{2,1,0:T(4,128)(2,1)} %bitcast.2) | data formatting | bytes 786432

commit v2 on v1

--- a/solution.py
+++ b/solution.py
@@ -1,4 +1,4 @@
-import functools
+import itertools
 
 import jax
 import jax.numpy as jnp
@@ -14,12 +14,14 @@
 SUB = 96
 CHUNK = 8
 NS = 128
-GROUPS = ((0, 0), (0, 1), (0, 3), (1, 0), (0, 2), (1, 1), (1, 3), (1, 2))
+AWAY = (0, 1, 3, 2)
+ZP = len(AWAY)
+WP = 1
 
 
 def kernel(
     a_in, w_in, blocks, rows, cols, out_ref,
-    a_src, a_all, id_all, w_all, wi_all, acc, wide, stage, id_own, wi_own, merged, info, table,
+    a_src, a_all, id_y, id_all, w_all, wi_all, acc, wide, stage, id_own, wi_own, merged, info, table,
     a0_send, a0_recv, z_send, z_recv, zi_send, zi_recv, d_send, d_recv,
     own_send, owni_send, w_recv, wi_recv, f_send, fi_send, out_send, out_recv, info_sem,
 ):
@@ -72,7 +74,7 @@
     a_local = []
     for b in range(2):
         a_local.append(pltpu.make_async_copy(a_src.at[b, pl.ds(y * SUB, SUB)], a_all.at[c, 2 * vir + b], a0_recv.at[0, b]))
-    a_local.append(pltpu.make_async_copy(id_own, id_all.at[vir], a0_recv.at[0, 2]))
+    a_local.append(pltpu.make_async_copy(id_own, id_y.at[y], a0_recv.at[0, 2]))
     for copy in a_local:
         copy.start()
     a0 = []
@@ -81,65 +83,74 @@
         for b in range(2):
             src = a_src.at[b, pl.ds(to * SUB, SUB)]
             a0.append(remote(src, a_all.at[c, 2 * vir + b], a0_send.at[k, b], a0_recv.at[k, b], dev(x, c, to, z)))
-        a0.append(remote(id_own, id_all.at[vir], a0_send.at[k, 2], a0_recv.at[k, 2], dev(x, c, to, z)))
+        a0.append(remote(id_own, id_y.at[y], a0_send.at[k, 2], a0_recv.at[k, 2], dev(x, c, to, z)))
     for copy in a0:
         copy.start()
 
     mine, mine_sem = w_all.at[oy, x, c], w_recv.at[oy, x, c]
     targets = (dev(x + 1, home, y, z), dev(x - 1, home, y, z), dev(x, home, y + 1, z), dev(x, home, y - 1, z))
     beside = dev(x, home, y, z)
-    w_src = [w_in.at[0, pl.ds(r * CHUNK, CHUNK)] for r in range(2)]
-
-    def own_tiles(r, d, to):
-        return remote(w_src[r], mine.at[r], own_send.at[r, d], mine_sem.at[r], to)
+    part = CHUNK // WP
+
+    def w_src(r, w):
+        return w_in.at[0, pl.ds(r * CHUNK + w * part, part)]
+
+    def own_tiles(r, w, d, to):
+        return remote(w_src(r, w), mine.at[r, w], own_send.at[r, w, d], mine_sem.at[r, w], to)
 
     def own_marks(d, to):
         return remote(wi_own, wi_all.at[oy, x, c], owni_send.at[d], wi_recv.at[oy, x, c], to)
 
-    def own_start(ds):
-        for r in range(2):
-            for d in ds:
-                own_tiles(r, d, targets[d]).start()
-                if r == 0:
-                    own_marks(d, targets[d]).start()
+    def own_start(ds, rs):
+        for r in rs:
+            for w in range(WP):
+                for d in ds:
+                    if r == 0 and w == 0:
+                        own_marks(d, targets[d]).start()
+                    own_tiles(r, w, d, targets[d]).start()
 
     def own_beside():
         @pl.when(unmatched == 0)
         def _():
             for r in range(2):
-                pltpu.make_async_copy(w_src[r], mine.at[r], mine_sem.at[r]).start()
+                for w in range(WP):
+                    pltpu.make_async_copy(w_src(r, w), mine.at[r, w], mine_sem.at[r, w]).start()
             pltpu.make_async_copy(wi_own, wi_all.at[oy, x, c], wi_recv.at[oy, x, c]).start()
 
         @pl.when(unmatched == 1)
         def _():
             for r in range(2):
-                own_tiles(r, 4, beside).start()
+                for w in range(WP):
+                    own_tiles(r, w, 4, beside).start()
             own_marks(4, beside).start()
 
     def zchunk(ref, zz, lo, n, per):
         return ref.at[pl.ds(lax.rem(zz + NZ, NZ) * per + lo, n)]
 
     def plan(way, h):
-        return [way] if h == NZ // 2 else [0, 1]
+        return range(way * ZP // 2, (way + 1) * ZP // 2) if h == NZ // 2 else range(ZP)
 
     def z_copy(way, h, q, arriving=False):
         s = 1 if way == 0 else -1
         from_z = z - s * (h if arriving else h - 1)
         to = dev(x, c, y, z + s)
-        chunk = zchunk(a_all.at[c], from_z, 4 * q, 4, 2 * NY)
+        chunk = zchunk(a_all.at[c], from_z, 2 * lax.rem(y - AWAY[q] + NY, NY), 2, 2 * NY)
         out = [remote(chunk, chunk, z_send.at[way, q, h - 1], z_recv.at[way, q, h - 1], to)]
-        if q == 0:
-            chunk = zchunk(id_all, from_z, 0, NY, NY)
+        if q == ZP - 1:
+            chunk = id_all.at[lax.rem(from_z + NZ, NZ)]
             out.append(remote(chunk, chunk, zi_send.at[way, h - 1], zi_recv.at[way, h - 1], to))
         return out
 
-    def d_copy(way, h, core, q):
+    def d_copy(way, h, core):
         s = 1 if way == 0 else -1
-        chunk = zchunk(a_all.at[core], z - s * h, 4 * q, 4, 2 * NY)
-        return remote(chunk, chunk, d_send.at[way, q, h], d_recv.at[way, q, h], dev(x, 1 - c, y, z))
+        chunk = zchunk(a_all.at[core], z - s * h, 0, 2 * NY, 2 * NY)
+        return remote(chunk, chunk, d_send.at[way, h], d_recv.at[way, h], dev(x, 1 - c, y, z))
+
+    def d_ways(h):
+        return range(1 if h in (0, NZ // 2) else 2)
 
     def z_step(h):
-        for q in range(2):
+        for q in range(ZP):
             for way in range(2):
                 if q not in plan(way, h):
                     continue
@@ -148,21 +159,22 @@
                 if h < NZ // 2 and q in plan(way, h + 1):
                     for copy in z_copy(way, h + 1, q):
                         copy.start()
-                d_copy(way, h, c, q).start()
+        for way in d_ways(h):
+            d_copy(way, h, c).start()
 
     nearest = (oy + unmatched) % 2
 
-    def forwards(j, dx, cs, r):
+    def forwards(j, dx, cs, r, w):
         o = nearest if j == 0 else 1 - nearest
         xs = lax.rem(x - dx + NX, NX)
         dy = lax.rem(y - (2 * c + o) + NY, NY)
-        slot, sem = w_all.at[o, xs, cs, r], w_recv.at[o, xs, cs, r]
+        slot, sem = w_all.at[o, xs, cs, r, w], w_recv.at[o, xs, cs, r, w]
         marks, marks_sem = wi_all.at[o, xs, cs], wi_recv.at[o, xs, cs]
 
         def send(d):
             to = (dev(x + 1, c, y, z), dev(x - 1, c, y, z), dev(x, c, y + 1, z), dev(x, c, y - 1, z))[d]
-            out = [remote(slot, slot, f_send.at[j, dx, cs, r, d], sem, to)]
-            if r == 0:
+            out = [remote(slot, slot, f_send.at[j, dx, cs, r, w, d], sem, to)]
+            if r == 0 and w == 0:
                 out.append(remote(marks, marks, fi_send.at[j, dx, cs, d], marks_sem, to))
             return out
 
@@ -193,22 +205,16 @@
             else:
                 pl.when(cond)(run)
 
-    def group(g):
-        j, dx = GROUPS[g]
-        o = nearest if j == 0 else 1 - nearest
-        xs = lax.rem(x - dx + NX, NX)
-        for r in range(2):
-            for cs in range(2):
-                landed(w_all.at[o, xs, cs, r], w_recv.at[o, xs, cs, r])
-                if r == 0:
-                    landed(wi_all.at[o, xs, cs], wi_recv.at[o, xs, cs])
-                each(forwards(j, dx, cs, r), lambda copy: copy.start())
-
-    def groups(which, *gs):
+    def take(which, *parts):
         @pl.when(unmatched == which)
         def _():
-            for g in gs:
-                group(g)
+            for w, (j, dx, r), cs in itertools.product(range(WP), parts, range(2)):
+                o = nearest if j == 0 else 1 - nearest
+                xs = lax.rem(x - dx + NX, NX)
+                landed(w_all.at[o, xs, cs, r, w], w_recv.at[o, xs, cs, r, w])
+                if r == 0 and w == 0:
+                    landed(wi_all.at[o, xs, cs], wi_recv.at[o, xs, cs])
+                each(forwards(j, dx, cs, r, w), lambda copy: copy.start())
 
     def product(o, p):
         marks = table[...]
@@ -226,14 +232,14 @@
                 col = info[p, 3, i * CHUNK + t]
                 s = jnp.minimum(info[p, row // TILE, row % TILE], NS - 1)
                 lhs.append(jnp.concatenate([a_all[k, s] for k in range(2)], axis=0))
-                tile = w_all[o, i // 4, (i // 2) % 2, i % 2, t]
+                tile = w_all[o, i // 4, (i // 2) % 2, i % 2, t // part, t % part]
                 rhs.append(jnp.concatenate([jnp.where(col == b, tile, jnp.zeros_like(tile)) for b in range(OBLK)], axis=1))
             left = jnp.concatenate(lhs, axis=1)
             right = jnp.concatenate(rhs, axis=0)
             acc[o] += jnp.dot(left, right, preferred_element_type=jnp.float32)
             return carry
 
-        lax.fori_loop(0, NX * 4, chunk, 0)
+        lax.fori_loop(0, NX * 4, chunk, 0, unroll=4)
 
     def out_copies(o, p, act):
         ys = 2 * c + o
@@ -256,77 +262,84 @@
             stage[p, k] = wide[pl.ds(0, SUB * OBLK), :].astype(jnp.bfloat16)
         out_copies(o, p, lambda copy, local: copy.start())
 
-    own_start((0, 1))
-    own_beside()
     for copy in a_local:
         copy.wait()
-    for k in (1, 3, 2):
+    for way in range(2):
+        for copy in z_copy(way, 1, 0):
+            copy.start()
+    own_start((0, 1), (0, 1))
+    own_start((2, 3), (1, 0))
+    own_beside()
+    for q in range(1, ZP):
+        k = AWAY[q]
         from_y = lax.rem(y - k + NY, NY) + z * NY
         for b in range(2):
             landed(a_all.at[c, 2 * from_y + b], a0_recv.at[k, b])
-        landed(id_all.at[from_y], a0_recv.at[k, 2])
-    for q in range(2):
+        landed(id_y.at[lax.rem(y - k + NY, NY)], a0_recv.at[k, 2])
+        if q == ZP - 1:
+            id_all[z] = id_y[0] + id_y[1] + id_y[2] + id_y[3]
         for way in range(2):
             for copy in z_copy(way, 1, q):
                 copy.start()
-    own_start((2, 3))
-    for q in range(2):
-        d_copy(0, 0, c, q).start()
-
-    groups(0, 0)
+    d_copy(0, 0, c).start()
+
     z_step(1)
-    groups(0, 1, 2, 3)
-    groups(1, 0)
-    for h in (2, 3, 4, 5):
-        z_step(h)
-    groups(0, 4, 5, 6)
-    groups(1, 1, 2, 3)
+    take(0, (0, 1, 0), (0, 3, 0), (1, 0, 1))
+    take(1, (0, 0, 1))
+    z_step(2)
+    take(0, (0, 1, 1), (0, 3, 1), (1, 0, 0))
+    take(1, (0, 0, 0))
+    z_step(3)
+    take(0, (0, 2, 0))
+    take(1, (1, 0, 1))
+    z_step(4)
+    take(0, (1, 1, 1), (1, 3, 1))
+    take(1, (0, 1, 1), (0, 3, 1))
+    z_step(5)
+    take(0, (1, 1, 0), (1, 3, 0))
+    take(1, (0, 1, 0), (0, 3, 0))
     z_step(6)
+    take(0, (1, 2, 0))
+    take(1, (0, 2, 0), (1, 1, 1), (1, 3, 1))
     z_step(7)
-    groups(0, 7)
-    groups(1, 4, 5, 6)
     z_step(8)
-    for q in range(2):
-        d_copy(0, 0, 1 - c, q).wait_recv()
-        for h in range(1, NZ // 2 + 1):
-            for way in range(2):
-                if q in plan(way, h):
-                    d_copy(way, h, 1 - c, q).wait_recv()
-
-    table[...] = lax.fori_loop(0, NY * NZ, lambda i, total: total + id_all[i], jnp.zeros((8, TILE), jnp.int32))
+    for h in range(NZ // 2 + 1):
+        for way in d_ways(h):
+            d_copy(way, h, 1 - c).wait_recv()
+
+    table[...] = lax.fori_loop(0, NZ, lambda i, total: total + id_all[i], jnp.zeros((8, TILE), jnp.int32))
     first = (nearest + 1 - unmatched) % 2
+    take(0, (1, 2, 1))
+    take(1, (0, 2, 1))
     product(first, 0)
     finish(first, 0)
-    groups(1, 7)
+    take(0, (0, 0, 0), (0, 0, 1), (0, 2, 1))
+    take(1, (1, 0, 0), (1, 1, 0), (1, 3, 0), (1, 2, 0), (1, 2, 1))
     product(1 - first, 1)
     finish(1 - first, 1)
 
     for copy in a0:
         copy.wait_send()
-    for r in range(2):
-        for d in range(4):
-            own_tiles(r, d, targets[d]).wait_send()
-            if r == 0:
-                own_marks(d, targets[d]).wait_send()
+    for d in range(4):
+        for r, w in itertools.product(range(2), range(WP)):
+            own_tiles(r, w, d, targets[d]).wait_send()
+        own_marks(d, targets[d]).wait_send()
 
     @pl.when(unmatched == 1)
     def _():
-        for r in range(2):
-            own_tiles(r, 4, beside).wait_send()
+        for r, w in itertools.product(range(2), range(WP)):
+            own_tiles(r, w, 4, beside).wait_send()
         own_marks(4, beside).wait_send()
 
-    for q in range(2):
-        d_copy(0, 0, c, q).wait_send()
-        for h in range(1, NZ // 2 + 1):
-            for way in range(2):
-                if q in plan(way, h):
-                    for copy in z_copy(way, h, q):
-                        copy.wait_send()
-                    d_copy(way, h, c, q).wait_send()
-    for j, dx in GROUPS:
-        for r in range(2):
-            for cs in range(2):
-                each(forwards(j, dx, cs, r), lambda copy: copy.wait_send())
+    for h in range(NZ // 2 + 1):
+        for way in d_ways(h):
+            d_copy(way, h, c).wait_send()
+        for way in range(2):
+            for q in plan(way, h) if h > 0 else ():
+                for copy in z_copy(way, h, q):
+                    copy.wait_send()
+    for j, dx, cs, r, w in itertools.product(range(2), range(NX), range(2), range(2), range(WP)):
+        each(forwards(j, dx, cs, r, w), lambda copy: copy.wait_send())
     for o, p in ((first, 0), (1 - first, 1)):
         out_copies(o, p, lambda copy, local: None if local else copy.wait_send())
     for k in range(NY):
@@ -350,8 +363,9 @@
         scratch_shapes=[
             vmem((2, NY * SUB, tile), jnp.bfloat16),
             vmem((2, NS, SUB, tile), jnp.bfloat16),
-            vmem((NY * NZ, 8, tile), jnp.int32),
-            vmem((2, NX, 2, 2, CHUNK, tile, tile), jnp.bfloat16),
+            vmem((NY, 8, tile), jnp.int32),
+            vmem((NZ, 8, tile), jnp.int32),
+            vmem((2, NX, 2, 2, WP, CHUNK // WP, tile, tile), jnp.bfloat16),
             vmem((2, NX, 2, 8, tile), jnp.int32),
             vmem((2, 2 * SUB, OBLK * tile), jnp.float32),
             vmem((2 * rows, tile), jnp.float32),
@@ -362,10 +376,10 @@
             smem((2, 8, tile), jnp.int32),
             vmem((8, tile), jnp.int32),
             dma((NY, 3)), dma((NY, 3)),
-            dma((2, 2, half)), dma((2, 2, half)), dma((2, half)), dma((2, half)),
-            dma((2, 2, half + 1)), dma((2, 2, half + 1)),
-            dma((2, 5)), dma((5,)), dma((2, NX, 2, 2)), dma((2, NX, 2)),
-            dma((2, NX, 2, 2, 4)), dma((2, NX, 2, 4)),
+            dma((2, ZP, half)), dma((2, ZP, half)), dma((2, half)), dma((2, half)),
+            dma((2, half + 1)), dma((2, half + 1)),
+            dma((2, WP, 5)), dma((5,)), dma((2, NX, 2, 2, WP)), dma((2, NX, 2)),
+            dma((2, NX, 2, 2, WP, 4)), dma((2, NX, 2, 4)),
             dma((2, 2)), dma((NY,)), dma((2,)),
         ],
         compiler_params=pltpu.CompilerParams(

time: 91.6 us -> 83.1 us (0.907)
  Pallas kernels: 89.6 us -> 81.1 us
    pallas_call x1, Pallas kernels: 89.6 us -> 81.1 us  [on_device(): pl.pallas_call(kernel, out_shape=jax.ShapeDtypeStruct((rows * OBLK, tile)...]
where the time goes in v2:
time: 83.1 us; the launch traced here: 83 us
  Pallas kernels  81.1 us (98%)
  local copies, waits for them, and re-layouts  1.88 us (2%)
    pallas_call x1, Pallas kernels, on_device(): pl.pallas_call(kernel, out_shape=jax.ShapeDtypeStruct((rows * OBLK, tile)...  81.1 us
    unnamed x1, local copies, waits for them, and re-layouts  1.88 us

profile of v2, /device:TPU:1, one launch (start us, length us, event | category | flops | bytes accessed | tf_op | source)
XLA Modules:
  0.0 83.0 jit_solution(865968939367242500)
XLA Ops:
  0.0 81.1 %shard_map.55 = bf16[1536,128]{1,0:T(8,128)(2,1)} custom-call(bf16[768,128]{1,0:T(8,128)(2,1)} %bitcast.3, bf16[1,16,128,128]{3,2,1,0:T(8,128)(2,1)} %w_in.1, s32[2]{0:T(128)} %blocks.1, s32[1,16]{1,0:T(1,128)} %rows.1, s32[1,16]{1,0:T(1,128)} %cols.1), custom_call_target="tpu_custom_call" | custom-call | tf_op jit(solution)/shard_map/pallas_call | solution.py:352
  81.1 1.9 %copy.7 = bf16[384,4,128]{2,1,0:T(4,128)(2,1)} copy(bf16[384,4,128]{2,1,0:T(4,128)(2,1)} %bitcast.2) | data formatting | bytes 786432

commit v3 on v2

--- a/solution.py
+++ b/solution.py
@@ -14,16 +14,15 @@
 SUB = 96
 CHUNK = 8
 NS = 128
-AWAY = (0, 1, 3, 2)
-ZP = len(AWAY)
+ZP = 2
 WP = 1
 
 
 def kernel(
     a_in, w_in, blocks, rows, cols, out_ref,
-    a_src, a_all, id_y, id_all, w_all, wi_all, acc, wide, stage, id_own, wi_own, merged, info, table,
+    a_vm, a_src, a_all, id_y, id_all, w_all, wi_all, acc, wide, stage, id_own, wi_own, merged, info, table,
     a0_send, a0_recv, z_send, z_recv, zi_send, zi_recv, d_send, d_recv,
-    own_send, owni_send, w_recv, wi_recv, f_send, fi_send, out_send, out_recv, info_sem,
+    own_send, owni_send, w_recv, wi_recv, f_send, fi_send, out_send, out_recv, info_sem, in_sem,
 ):
     occ, vir = lax.axis_index("occ"), lax.axis_index("vir")
     x, c = occ // 2, lax.rem(occ, 2)
@@ -50,7 +49,11 @@
     for p in partners:
         pl.semaphore_signal(barrier, inc=1, device_id=p, device_id_type=MESH)
 
-    wide[...] = a_in[...].astype(jnp.float32)
+    fetch = pltpu.make_async_copy(a_in, a_vm, in_sem)
+    fetch.start()
+
+    fetch.wait()
+    wide[...] = a_vm[...].astype(jnp.float32)
     for b in range(2):
         a_src[b] = wide[pl.ds(b, NY * SUB, stride=2), :].astype(jnp.bfloat16)
     sub = lax.broadcasted_iota(jnp.int32, (8, TILE), 0)
@@ -71,19 +74,19 @@
 
     pl.semaphore_wait(barrier, len(partners))
 
-    a_local = []
-    for b in range(2):
-        a_local.append(pltpu.make_async_copy(a_src.at[b, pl.ds(y * SUB, SUB)], a_all.at[c, 2 * vir + b], a0_recv.at[0, b]))
-    a_local.append(pltpu.make_async_copy(id_own, id_y.at[y], a0_recv.at[0, 2]))
+    a_local = [
+        pltpu.make_async_copy(a_src.at[:, pl.ds(y * SUB, SUB)], a_all.at[c, pl.ds(2 * NY * z, 2)], a0_recv.at[0, 0]),
+        pltpu.make_async_copy(id_own, id_y.at[0], a0_recv.at[0, 1]),
+    ]
     for copy in a_local:
         copy.start()
     a0 = []
     for k in (1, 3, 2):
         to = lax.rem(y + k, NY)
-        for b in range(2):
-            src = a_src.at[b, pl.ds(to * SUB, SUB)]
-            a0.append(remote(src, a_all.at[c, 2 * vir + b], a0_send.at[k, b], a0_recv.at[k, b], dev(x, c, to, z)))
-        a0.append(remote(id_own, id_y.at[y], a0_send.at[k, 2], a0_recv.at[k, 2], dev(x, c, to, z)))
+        src, dst = a_src.at[:, pl.ds(to * SUB, SUB)], a_all.at[c, pl.ds(2 * NY * z + 2 * k, 2)]
+        a0.append(remote(src, dst, a0_send.at[k, 0], a0_recv.at[k, 0], dev(x, c, to, z)))
+    for k in (1, 3, 2):
+        a0.append(remote(id_own, id_y.at[k], a0_send.at[k, 1], a0_recv.at[k, 1], dev(x, c, lax.rem(y + k, NY), z)))
     for copy in a0:
         copy.start()
 
@@ -134,7 +137,7 @@
         s = 1 if way == 0 else -1
         from_z = z - s * (h if arriving else h - 1)
         to = dev(x, c, y, z + s)
-        chunk = zchunk(a_all.at[c], from_z, 2 * lax.rem(y - AWAY[q] + NY, NY), 2, 2 * NY)
+        chunk = zchunk(a_all.at[c], from_z, q * 2 * NY // ZP, 2 * NY // ZP, 2 * NY)
         out = [remote(chunk, chunk, z_send.at[way, q, h - 1], z_recv.at[way, q, h - 1], to)]
         if q == ZP - 1:
             chunk = id_all.at[lax.rem(from_z + NZ, NZ)]
@@ -239,7 +242,7 @@
             acc[o] += jnp.dot(left, right, preferred_element_type=jnp.float32)
             return carry
 
-        lax.fori_loop(0, NX * 4, chunk, 0, unroll=4)
+        lax.fori_loop(0, NX * 4, chunk, 0, unroll=8)
 
     def out_copies(o, p, act):
         ys = 2 * c + o
@@ -264,19 +267,15 @@
 
     for copy in a_local:
         copy.wait()
-    for way in range(2):
-        for copy in z_copy(way, 1, 0):
-            copy.start()
     own_start((0, 1), (0, 1))
     own_start((2, 3), (1, 0))
     own_beside()
-    for q in range(1, ZP):
-        k = AWAY[q]
-        from_y = lax.rem(y - k + NY, NY) + z * NY
-        for b in range(2):
-            landed(a_all.at[c, 2 * from_y + b], a0_recv.at[k, b])
-        landed(id_y.at[lax.rem(y - k + NY, NY)], a0_recv.at[k, 2])
+    for q in range(ZP):
+        for k in ((1,), (3, 2))[q]:
+            landed(a_all.at[c, pl.ds(2 * NY * z + 2 * k, 2)], a0_recv.at[k, 0])
         if q == ZP - 1:
+            for k in (1, 3, 2):
+                landed(id_y.at[k], a0_recv.at[k, 1])
             id_all[z] = id_y[0] + id_y[1] + id_y[2] + id_y[3]
         for way in range(2):
             for copy in z_copy(way, 1, q):
@@ -290,24 +289,27 @@
     take(0, (0, 1, 1), (0, 3, 1), (1, 0, 0))
     take(1, (0, 0, 0))
     z_step(3)
+    z_step(4)
     take(0, (0, 2, 0))
     take(1, (1, 0, 1))
-    z_step(4)
+    z_step(5)
     take(0, (1, 1, 1), (1, 3, 1))
     take(1, (0, 1, 1), (0, 3, 1))
-    z_step(5)
     take(0, (1, 1, 0), (1, 3, 0))
     take(1, (0, 1, 0), (0, 3, 0))
     z_step(6)
+    z_step(7)
+    z_step(8)
     take(0, (1, 2, 0))
     take(1, (0, 2, 0), (1, 1, 1), (1, 3, 1))
-    z_step(7)
-    z_step(8)
     for h in range(NZ // 2 + 1):
         for way in d_ways(h):
             d_copy(way, h, 1 - c).wait_recv()
 
-    table[...] = lax.fori_loop(0, NZ, lambda i, total: total + id_all[i], jnp.zeros((8, TILE), jnp.int32))
+    slot = lax.fori_loop(0, NZ, lambda i, total: total + id_all[i], jnp.zeros((8, TILE), jnp.int32))
+    slot = jnp.minimum(slot, NS - 1)
+    come = (y + NY - slot % (2 * NY) // 2) % NY
+    table[...] = jnp.where(sub < 2, slot // (2 * NY) * (2 * NY) + 2 * come + slot % 2, 0)
     first = (nearest + 1 - unmatched) % 2
     take(0, (1, 2, 1))
     take(1, (0, 2, 1))
@@ -353,14 +355,15 @@
         kernel,
         out_shape=jax.ShapeDtypeStruct((rows * OBLK, tile), jnp.bfloat16),
         in_specs=[
-            pl.BlockSpec(memory_space=vmem),
+            pl.BlockSpec(memory_space=pl.ANY),
             pl.BlockSpec(memory_space=pl.ANY),
             pl.BlockSpec(memory_space=smem),
             pl.BlockSpec(memory_space=smem),
             pl.BlockSpec(memory_space=smem),
         ],
-        out_specs=pl.BlockSpec(memory_space=vmem),
+        out_specs=pl.BlockSpec(memory_space=pl.ANY),
         scratch_shapes=[
+            vmem((2 * rows, tile), jnp.bfloat16),
             vmem((2, NY * SUB, tile), jnp.bfloat16),
             vmem((2, NS, SUB, tile), jnp.bfloat16),
             vmem((NY, 8, tile), jnp.int32),
@@ -375,12 +378,12 @@
             vmem((2, 8, tile), jnp.int32),
             smem((2, 8, tile), jnp.int32),
             vmem((8, tile), jnp.int32),
-            dma((NY, 3)), dma((NY, 3)),
+            dma((NY, 2)), dma((NY, 2)),
             dma((2, ZP, half)), dma((2, ZP, half)), dma((2, half)), dma((2, half)),
             dma((2, half + 1)), dma((2, half + 1)),
             dma((2, WP, 5)), dma((5,)), dma((2, NX, 2, 2, WP)), dma((2, NX, 2)),
             dma((2, NX, 2, 2, WP, 4)), dma((2, NX, 2, 4)),
-            dma((2, 2)), dma((NY,)), dma((2,)),
+            dma((2, 2)), dma((NY,)), dma((2,)), dma,
         ],
         compiler_params=pltpu.CompilerParams(
             collective_id=0, has_side_effects=True, vmem_limit_bytes=56 << 20

time: 83.1 us -> 79.2 us (0.953)
  Pallas kernels: 81.1 us -> 77.2 us
    pallas_call x1, Pallas kernels: 81.1 us -> 77.2 us  [on_device(): pl.pallas_call(kernel, out_shape=jax.ShapeDtypeStruct((rows * OBLK, tile)...]
where the time goes in v3:
time: 79.2 us; the launch traced here: 79 us
  Pallas kernels  77.2 us (97%)
  local copies, waits for them, and re-layouts  1.88 us (2%)
    pallas_call x1, Pallas kernels, on_device(): pl.pallas_call(kernel, out_shape=jax.ShapeDtypeStruct((rows * OBLK, tile)...  77.2 us
    unnamed x1, local copies, waits for them, and re-layouts  1.88 us

profile of v3, /device:TPU:1, one launch (start us, length us, event | category | flops | bytes accessed | tf_op | source)
XLA Modules:
  0.0 79.0 jit_solution(4541039467171678541)
XLA Ops:
  0.0 77.2 %shard_map.55 = bf16[1536,128]{1,0:T(8,128)(2,1)} custom-call(bf16[768,128]{1,0:T(8,128)(2,1)} %bitcast.3, bf16[1,16,128,128]{3,2,1,0:T(8,128)(2,1)} %w_in.1, s32[2]{0:T(128)} %blocks.1, s32[1,16]{1,0:T(1,128)} %rows.1, s32[1,16]{1,0:T(1,128)} %cols.1), custom_call_target="tpu_custom_call" | custom-call | tf_op jit(solution)/shard_map/pallas_call | solution.py:354
  77.2 1.9 %copy.7 = bf16[384,4,128]{2,1,0:T(4,128)(2,1)} copy(bf16[384,4,128]{2,1,0:T(4,128)(2,1)} %bitcast.2) | data formatting | bytes 786432

commit v4 on v3

--- a/solution.py
+++ b/solution.py
@@ -299,9 +299,9 @@
     take(1, (0, 1, 0), (0, 3, 0))
     z_step(6)
     z_step(7)
-    z_step(8)
     take(0, (1, 2, 0))
     take(1, (0, 2, 0), (1, 1, 1), (1, 3, 1))
+    z_step(8)
     for h in range(NZ // 2 + 1):
         for way in d_ways(h):
             d_copy(way, h, 1 - c).wait_recv()

time: 79.2 us -> 77.7 us (0.981)
  Pallas kernels: 77.2 us -> 75.7 us
    pallas_call x1, Pallas kernels: 77.2 us -> 75.7 us  [on_device(): pl.pallas_call(kernel, out_shape=jax.ShapeDtypeStruct((rows * OBLK, tile)...]
where the time goes in v4:
time: 77.7 us; the launch traced here: 77.5 us
  Pallas kernels  75.7 us (97%)
  local copies, waits for them, and re-layouts  1.88 us (2%)
    pallas_call x1, Pallas kernels, on_device(): pl.pallas_call(kernel, out_shape=jax.ShapeDtypeStruct((rows * OBLK, tile)...  75.7 us
    unnamed x1, local copies, waits for them, and re-layouts  1.88 us

profile of v4, /device:TPU:1, one launch (start us, length us, event | category | flops | bytes accessed | tf_op | source)
XLA Modules:
  0.0 77.5 jit_solution(9282974974379841551)
XLA Ops:
  0.0 75.7 %shard_map.55 = bf16[1536,128]{1,0:T(8,128)(2,1)} custom-call(bf16[768,128]{1,0:T(8,128)(2,1)} %bitcast.3, bf16[1,16,128,128]{3,2,1,0:T(8,128)(2,1)} %w_in.1, s32[2]{0:T(128)} %blocks.1, s32[1,16]{1,0:T(1,128)} %rows.1, s32[1,16]{1,0:T(1,128)} %cols.1), custom_call_target="tpu_custom_call" | custom-call | tf_op jit(solution)/shard_map/pallas_call | solution.py:354
  75.7 1.9 %copy.7 = bf16[384,4,128]{2,1,0:T(4,128)(2,1)} copy(bf16[384,4,128]{2,1,0:T(4,128)(2,1)} %bitcast.2) | data formatting | bytes 786432
